TPU v7x, 32 devices: a whole 2x2x4 slice. The times are simulated.
32 devices in a mesh: clip: 8 (over y, x, core), row: 4 (over z).
Axes of the slice: x: 2, y: 2, z: 4, core: 2. Of those that a mesh axis runs over, the one named last changes fastest.
Arguments:
- video_clips: bfloat16 [8, 4, 16, 64, 512], P('clip', None, 'row'), may hold values from -60 to 60
- norm_gain: float32 [512], replicated, may hold values from 0.1 to 1.9
- norm_bias: float32 [512], replicated, may hold values from -3 to 3
- spatial_weight: bfloat16 [4608, 512], P('clip'), may hold values from -0.09375 to 0.09375
- spatial_bias: float32 [512], replicated, may hold values from -3 to 3
- temporal_weight: bfloat16 [1536, 512], P('clip'), may hold values from -0.15625 to 0.15625
- temporal_bias: float32 [512], replicated, may hold values from -3 to 3
Outputs:
- encoded: bfloat16 [8, 2, 16, 64, 512], P('clip', None, 'row')
All inputs are finite; a program needn't handle non-finite values.
Results may differ from a plain program's by a relative error of at most 0.0025.
Values may be sent and summed in bfloat16 or wider, within the bound.
A program may use at most 64 MiB of HBM per device.

v0:
```python
import jax
import jax.numpy as jnp
from jax import lax
from jax.sharding import PartitionSpec as P

GROUPS = 32


def extended(cells, sides, width):
    for axis, dim in sides:
        count = lax.axis_size(axis)
        ends = count - 1
        head = lax.slice_in_dim(cells, 0, width, axis=dim)
        tail = lax.slice_in_dim(cells, cells.shape[dim] - width, cells.shape[dim], axis=dim)
        cells = jnp.concatenate(
            [
                lax.ppermute(tail, axis, [(i, (i + 1) % count) for i in range(ends)]),
                cells,
                lax.ppermute(head, axis, [((i + 1) % count, i) for i in range(ends)]),
            ],
            axis=dim,
        )
    return cells


def body(
    video_clips, norm_gain, norm_bias, spatial_weight, spatial_bias, temporal_weight, temporal_bias
):
    clip_count, frames, row_count, col_count, channels = video_clips.shape
    group_width = channels // GROUPS
    population = frames * row_count * lax.axis_size("row") * col_count * group_width
    spatial_full, temporal_full = (
        lax.all_gather(spatial_weight, "clip", axis=0, tiled=True),
        lax.all_gather(temporal_weight, "clip", axis=0, tiled=True),
    )
    widened = video_clips.astype(jnp.float32)
    grouped = widened.reshape(clip_count, -1, GROUPS, group_width)
    group_mean = lax.psum(jnp.sum(grouped, axis=(1, 3)), "row") / population
    centered = grouped - group_mean[:, None, :, None]
    group_spread = lax.psum(jnp.sum(centered * centered, axis=(1, 3)), "row") / population
    inverse = lax.rsqrt(group_spread + 1e-06)
    mean_chan = jnp.repeat(group_mean, group_width, axis=1)[:, None, None, None, :]
    inverse_chan = jnp.repeat(inverse, group_width, axis=1)[:, None, None, None, :]
    normed = (widened - mean_chan) * inverse_chan * norm_gain + norm_bias
    activated = jax.nn.silu(normed).astype(jnp.bfloat16)
    padded = extended(activated, (("row", 2),), 1)
    padded = jnp.pad(padded, ((0, 0), (0, 0), (0, 0), (1, 1), (0, 0)))
    accum = jnp.zeros((clip_count * frames * row_count * col_count, channels), jnp.float32)
    for row_shift in range(3):
        for col_shift in range(3):
            tap_index = 3 * row_shift + col_shift
            window = padded[
                :, :, row_shift : row_shift + row_count, col_shift : col_shift + col_count
            ].reshape(-1, channels)
            accum = accum + jnp.dot(
                window,
                spatial_full[tap_index * channels : (tap_index + 1) * channels],
                preferred_element_type=jnp.float32,
            )
    middle = (
        (accum + spatial_bias)
        .astype(jnp.bfloat16)
        .reshape(clip_count, frames, row_count, col_count, channels)
    )
    time_padded = jnp.concatenate([middle[:, :1], middle[:, :1], middle], axis=1)
    result = jnp.zeros((clip_count * (frames // 2) * row_count * col_count, channels), jnp.float32)
    for tap_index in range(3):
        window = time_padded[:, tap_index : tap_index + frames : 2].reshape(-1, channels)
        result = result + jnp.dot(
            window,
            temporal_full[tap_index * channels : (tap_index + 1) * channels],
            preferred_element_type=jnp.float32,
        )
    input_padded = jnp.concatenate([widened[:, :1], widened], axis=1)
    pooled = 0.5 * (input_padded[:, 0:frames:2] + input_padded[:, 1 : frames + 1 : 2])
    result = (
        result.reshape(clip_count, frames // 2, row_count, col_count, channels)
        + temporal_bias
        + pooled
    )
    return result.astype(jnp.bfloat16)


def solution(mesh):
    placed = (
        P("clip", None, "row", None, None),
        P(),
        P(),
        P("clip", None),
        P(),
        P("clip", None),
        P(),
    )
    return jax.shard_map(
        body,
        mesh=mesh,
        in_specs=placed,
        out_specs=P("clip", None, "row", None, None),
        check_vma=False,
    )
```

profile of v0, /device:TPU:0, one launch (start us, length us, event | category | flops | bytes accessed | tf_op | source)
XLA Modules:
  0.0 91.4 jit_solution(348529516000516637)
XLA Ops:
  6.5 0.0 all-gather.3.cloned.1.call-start
  6.5 0.7 all-gather.3.cloned.1.call-update
  7.3 0.0 all-gather.5.cloned.1.call-start
  7.3 1.4 %convert_reduce_fusion = f32[512]{0:T(512)S(1)} fusion(bf16[1,4,4,64,512]{4,3,2,1,0:T(8,128)(2,1)} %param.7), kind=kLoop, calls=%fused_computation.13 | loop fusion | flops 1048064 | bytes 1050624 | tf_op jit(solution)/shard_map/reduce_sum | solution.py:38
  8.7 0.1 reduce_sum.26
  8.8 0.1 reduce_sum.30
  8.9 13.5 %psum.14 = f32[1,32]{1,0:T(1,128)S(1)} all-reduce(f32[1,32]{1,0:T(1,128)S(1)} %bitcast.49), channel_id=1, replica_groups=mesh['clip'=8,'row'=4] {'row'}, use_global_device_ids=true, to_apply=%region_2.0 | all-reduce | flops 32 | bytes 256 | tf_op jit(solution)/shard_map/psum | solution.py:38
  22.4 0.1 broadcast_in_dim.15
  22.5 0.1 broadcast_in_dim.16
  22.6 0.0 copy-done
  22.6 0.3 multiply_reduce_fusion
  22.9 0.1 reduce_sum.41
  23.0 0.1 reduce_sum.42
  23.1 8.4 %psum.15 = f32[1,32]{1,0:T(1,128)S(1)} all-reduce(f32[1,32]{1,0:T(1,128)S(1)} %bitcast.48), channel_id=1, replica_groups=mesh['clip'=8,'row'=4] {'row'}, use_global_device_ids=true, to_apply=%region_5.6 | all-reduce | flops 32 | bytes 256 | tf_op jit(solution)/shard_map/psum | solution.py:40
  31.5 0.1 broadcast_in_dim.17
  31.6 0.1 broadcast_in_dim.18
  31.7 0.0 copy-done.15
  31.7 0.0 copy-done.14
  31.7 0.7 multiply_convert_fusion
  32.4 3.9 %collective-permute-start = (bf16[1,4,1,64,512]{4,3,2,1,0:T(8,128)(2,1)S(1)}, bf16[1,4,1,64,512]{4,3,2,1,0:T(8,128)(2,1)S(1)}, u32[]{:S(2)}, u32[]{:S(2)}) collective-permute-start(bf16[1,4,1,64,512]{4,3,2,1,0:T(8,128)(2,1)S(1)} %get-tuple-element.15), channel_id=1, source_target_pairs={{0,1},{1,2},{2,3},{4,5},{5,6},{6,7},{8,9},{9,10},{10,11},{12,13},{... | collective-permute-start | bytes 786440 | tf_op jit(solution)/shard_map/ppermute | solution.py:17
  36.3 1.3 %collective-permute-start.1 = (bf16[1,4,1,64,512]{4,3,2,1,0:T(8,128)(2,1)S(1)}, bf16[1,4,1,64,512]{4,3,2,1,0:T(8,128)(2,1)S(1)}, u32[]{:S(2)}, u32[]{:S(2)}) collective-permute-start(bf16[1,4,1,64,512]{4,3,2,1,0:T(8,128)(2,1)S(1)} %get-tuple-element.16), channel_id=1, source_target_pairs={{1,0},{2,1},{3,2},{5,4},{6,5},{7,6},{9,8},{10,9},{11,10},{13,12},{... | collective-permute-start | bytes 786440 | tf_op jit(solution)/shard_map/ppermute | solution.py:19
  37.6 0.0 all-gather.5.cloned.1.call-update
  37.7 0.3 convert_element_type.14
  37.9 0.0 copy-start.1
  38.0 0.1 slice.144
  38.0 1.9 %pad_maximum_fusion = f32[1,5,4,64,512]{4,3,2,1,0:T(8,128)} fusion(f32[1,4,4,64,512]{4,3,2,1,0:T(8,128)S(1)} %convert_element_type.14, f32[1,1,4,64,512]{4,3,2,1,0:T(8,128)S(1)} %slice.144), kind=kLoop, calls=%fused_computation.3 | loop fusion | flops 655360 | bytes 5242880 | tf_op jit(solution)/shard_map/concatenate | solution.py:74
  39.9 0.3 copy-done.1
  40.2 0.0 collective-permute-done
  40.2 4.4 %collective-permute-done.1 = bf16[1,4,1,64,512]{4,3,2,1,0:T(8,128)(2,1)S(1)} collective-permute-done((bf16[1,4,1,64,512]{4,3,2,1,0:T(8,128)(2,1)S(1)}, bf16[1,4,1,64,512]{4,3,2,1,0:T(8,128)(2,1)S(1)}, u32[]{:S(2)}, u32[]{:S(2)}) %collective-permute-start.1) | collective-permute-done | bytes 262176 | tf_op jit(solution)/shard_map/ppermute | solution.py:19
  44.6 0.7 copy-done.10
  45.3 0.9 %fusion.5 = bf16[1,4,6,66,512]{4,3,2,1,0:T(8,128)(2,1)S(1)} fusion(bf16[1,4,1,64,512]{4,3,2,1,0:T(8,128)(2,1)S(1)} %collective-permute-done.1, bf16[1,4,4,64,512]{4,3,2,1,0:T(8,128)(2,1)S(1)} %multiply_convert_fusion, bf16[1,4,1,64,512]{4,3,2,1,0:T(8,128)(2,1)S(1)} %collective-permute-done), kind=kLoop, calls=%fused_computation.11 | loop fusion | flops 9732096 | bytes 3194880 | tf_op jit(solution)/shard_map/concatenate | solution.py:15
  46.2 0.0 copy-start.11
  46.3 3.2 %fusion.30 = (bf16[1,4,4,64,512]{4,3,2,1,0:T(8,128)(2,1)S(1)}, bf16[1,4,4,64,512]{4,3,2,1,0:T(8,128)(2,1)}, bf16[1,4,4,64,512]{4,3,2,1,0:T(8,128)(2,1)}, bf16[1,...) fusion(bf16[1,4,6,66,512]{4,3,2,1,0:T(8,128)(2,1)S(1)} %fusion.5), kind=kLoop, calls=%fused_computation.43 | loop fusion | bytes 12582912 | tf_op jit(solution)/shard_map/slice | solution.py:52
  49.4 0.0 copy-done.11
  49.4 1.5 %pad_maximum_fusion.3 = (bf16[1,4,4,64,512]{4,3,2,1,0:T(8,128)(2,1)}, bf16[1,4,4,64,512]{4,3,2,1,0:T(8,128)(2,1)}) fusion(bf16[1,4,4,64,512]{4,3,2,1,0:T(8,128)(2,1)S(1)} %multiply_convert_fusion, bf16[1,4,1,64,512]{4,3,2,1,0:T(8,128)(2,1)S(1)} %collective-permute-done, bf16[1,4,1,64,512]{4,3,2,1,0:T(8,128)(2,1)S(1)} %copy-done.11), kind=kLoop, calls=%fused_computation.17 | loop fusion | flops 1048576 | bytes 3670016 | tf_op jit(solution)/shard_map/concatenate | solution.py:15
  51.0 2.2 %fusion.16 = f32[1024,512]{1,0:T(8,128)S(1)} fusion(bf16[1024,512]{1,0:T(8,128)(2,1)} %bitcast.43, bf16[4608,512]{1,0:T(8,128)(2,1)} %all-gather.3.cloned.1.call-done), kind=kOutput, calls=%fused_computation.27 | convolution fusion | flops 536870912 | bytes 3670016 | tf_op jit(solution)/shard_map/dot_general | solution.py:55
  53.2 0.0 copy-start.6
  53.2 0.0 copy-done.8
  53.2 1.8 %fusion.18 = f32[1024,512]{1,0:T(8,128)S(1)} fusion(bf16[1024,512]{1,0:T(8,128)(2,1)S(1)} %bitcast.42, bf16[4608,512]{1,0:T(8,128)(2,1)} %all-gather.3.cloned.1.call-done), kind=kOutput, calls=%fused_computation.29 | convolution fusion | flops 536870912 | bytes 3670016 | tf_op jit(solution)/shard_map/dot_general | solution.py:55
  55.1 0.0 copy-done.3
  55.1 0.0 copy-done.6
  55.1 0.7 fusion.22
  55.8 0.5 copy-done.4
  56.3 0.7 fusion.24
  57.0 0.7 fusion.28
  57.7 0.0 copy-start.5
  57.7 0.5 copy-done.7
  58.2 0.7 fusion.14
  58.9 0.1 copy-done.5
  59.0 0.7 fusion.26
  59.7 0.0 copy-start.12
  59.7 0.7 fusion.20
  60.4 0.0 copy-done.12
  60.4 1.2 %add_convert_fusion = bf16[1024,512]{1,0:T(8,128)(2,1)S(1)} fusion(f32[1024,512]{1,0:T(8,128)S(1)} %fusion.14, f32[1024,512]{1,0:T(8,128)S(1)} %fusion.16, f32[1024,512]{1,0:T(8,128)S(1)} %fusion.18, f32[1024,512]{1,0:T(8,128)S(1)} %fusion.20, f32[1024,512]{1,0:T(8,128)S(1)} %fusion.22, f32[1024,512]{1,0:T(8,128)S(1)} %fusion.24, ...), kind=kOutput, calls=%fused_computation.4 | convolution fusion | flops 542113792 | bytes 19400704 | tf_op jit(solution)/shard_map/dot_general | solution.py:55
  61.7 0.1 pad_maximum_fusion.1
  61.9 0.1 fusion.31
  62.0 16.6 %all-gather.5.cloned.1.call-done = bf16[1536,512]{1,0:T(8,128)(2,1)} async-done(((bf16[192,512]{1,0:T(8,128)(2,1)}), bf16[1536,512]{1,0:T(8,128)(2,1)}) %all-gather.5.cloned.1.call-update) | async-done | bytes 1572880 | tf_op jit(solution)/shard_map/all_gather | solution.py:34
  78.5 1.6 %fusion.8 = f32[512,512]{1,0:T(8,128)S(1)} fusion(bf16[512,512]{1,0:T(8,128)(2,1)S(1)} %bitcast.47, bf16[1536,512]{1,0:T(8,128)(2,1)} %all-gather.5.cloned.1.call-done), kind=kOutput, calls=%fused_computation.21 | convolution fusion | flops 268435456 | bytes 2097152 | tf_op jit(solution)/shard_map/dot_general | solution.py:69
  80.1 0.4 convolution_add_fusion.1
  80.6 0.0 copy-start.13
  80.6 0.4 convolution_add_fusion
  81.0 1.1 %copy-done.2 = f32[1,4,4,64,512]{4,3,2,1,0:T(8,128)S(1)} copy-done((f32[1,4,4,64,512]{4,3,2,1,0:T(8,128)S(1)}, f32[1,4,4,64,512]{4,3,2,1,0:T(8,128)}, u32[]{:S(2)}) %copy-start.2) | copy-done | bytes 2097176
  82.2 0.0 copy-done.13
  82.2 2.4 %add_convert_fusion.1 = bf16[1,2,4,64,512]{4,3,2,1,0:T(8,128)(2,1)} fusion(f32[1,4,4,64,512]{4,3,2,1,0:T(8,128)S(1)} %copy-done.2, f32[1,5,4,64,512]{4,3,2,1,0:T(8,128)} %pad_maximum_fusion, f32[1,2,4,64,512]{4,3,2,1,0:T(8,128)S(1)} %bitcast.44, f32[512]{0:T(512)S(1)} %copy-done.13), kind=kLoop, calls=%fused_computation.18 | loop fusion | flops 1310720 | bytes 3672064 | tf_op jit(solution)/shard_map/convert_element_type | solution.py:81
  (17 shorter events, 0.1 us)
Async XLA Ops:
  6.5 16.0 %copy-start = (bf16[1,4,4,64,512]{4,3,2,1,0:T(8,128)(2,1)S(1)}, bf16[1,4,4,64,512]{4,3,2,1,0:T(8,128)(2,1)}, u32[]{:S(2)}) copy-start(bf16[1,4,4,64,512]{4,3,2,1,0:T(8,128)(2,1)} %param.7) | copy-start | bytes 3145732
  6.5 25.1 %copy-start.15 = (f32[512]{0:T(512)S(1)}, f32[512]{0:T(512)}, u32[]{:S(2)}) copy-start(f32[512]{0:T(512)} %param.8) | copy-start | bytes 6148
  6.5 25.1 %copy-start.14 = (f32[512]{0:T(512)S(1)}, f32[512]{0:T(512)}, u32[]{:S(2)}) copy-start(f32[512]{0:T(512)} %param.9) | copy-start | bytes 6148
  6.5 44.4 %all-gather.3.cloned.1.call-start = ((), (), s32[]{:S(2)}) async-start(), calls=%async_computation | async-start | bytes 5308416 | tf_op jit(solution)/shard_map/all_gather | solution.py:33
  7.3 71.2 %all-gather.5.cloned.1.call-start = ((), (), s32[]{:S(2)}) async-start(), calls=%async_computation.1 | async-start | bytes 1769472 | tf_op jit(solution)/shard_map/all_gather | solution.py:34
  32.4 7.8 %collective-permute-start = (bf16[1,4,1,64,512]{4,3,2,1,0:T(8,128)(2,1)S(1)}, bf16[1,4,1,64,512]{4,3,2,1,0:T(8,128)(2,1)S(1)}, u32[]{:S(2)}, u32[]{:S(2)}) collective-permute-start(bf16[1,4,1,64,512]{4,3,2,1,0:T(8,128)(2,1)S(1)} %get-tuple-element.15), channel_id=1, source_target_pairs={{0,1},{1,2},{2,3},{4,5},{5,6},{6,7},{8,9},{9,10},{10,11},{12,13},{... | collective-permute-start | bytes 786440 | tf_op jit(solution)/shard_map/ppermute | solution.py:17
  36.3 8.3 %collective-permute-start.1 = (bf16[1,4,1,64,512]{4,3,2,1,0:T(8,128)(2,1)S(1)}, bf16[1,4,1,64,512]{4,3,2,1,0:T(8,128)(2,1)S(1)}, u32[]{:S(2)}, u32[]{:S(2)}) collective-permute-start(bf16[1,4,1,64,512]{4,3,2,1,0:T(8,128)(2,1)S(1)} %get-tuple-element.16), channel_id=1, source_target_pairs={{1,0},{2,1},{3,2},{5,4},{6,5},{7,6},{9,8},{10,9},{11,10},{13,12},{... | collective-permute-start | bytes 786440 | tf_op jit(solution)/shard_map/ppermute | solution.py:19
  37.9 2.3 %copy-start.1 = (f32[1,4,4,64,512]{4,3,2,1,0:T(8,128)}, f32[1,4,4,64,512]{4,3,2,1,0:T(8,128)S(1)}, u32[]{:S(2)}) copy-start(f32[1,4,4,64,512]{4,3,2,1,0:T(8,128)S(1)} %convert_element_type.14) | copy-start | bytes 6291460
  44.6 0.7 copy-start.10
  46.2 3.2 %copy-start.11 = (bf16[1,4,1,64,512]{4,3,2,1,0:T(8,128)(2,1)S(1)}, bf16[1,4,1,64,512]{4,3,2,1,0:T(8,128)(2,1)}, u32[]{:S(2)}) copy-start(bf16[1,4,1,64,512]{4,3,2,1,0:T(8,128)(2,1)} %copy-done.10) | copy-start | bytes 786436
  51.0 2.2 %copy-start.8 = (bf16[1,4,4,64,512]{4,3,2,1,0:T(8,128)(2,1)S(1)}, bf16[1,4,4,64,512]{4,3,2,1,0:T(8,128)(2,1)}, u32[]{:S(2)}) copy-start(bf16[1,4,4,64,512]{4,3,2,1,0:T(8,128)(2,1)} %get-tuple-element.7) | copy-start | bytes 3145732
  51.0 4.1 %copy-start.3 = (bf16[4608,512]{1,0:T(8,128)(2,1)S(1)}, bf16[4608,512]{1,0:T(8,128)(2,1)}, u32[]{:S(2)}) copy-start(bf16[4608,512]{1,0:T(8,128)(2,1)} %all-gather.3.cloned.1.call-done) | copy-start | bytes 14155780
  53.2 1.9 %copy-start.6 = (bf16[1,4,4,64,512]{4,3,2,1,0:T(8,128)(2,1)S(1)}, bf16[1,4,4,64,512]{4,3,2,1,0:T(8,128)(2,1)}, u32[]{:S(2)}) copy-start(bf16[1,4,4,64,512]{4,3,2,1,0:T(8,128)(2,1)} %get-tuple-element.8) | copy-start | bytes 3145732
  55.0 1.2 %copy-start.4 = (bf16[1,4,4,64,512]{4,3,2,1,0:T(8,128)(2,1)S(1)}, bf16[1,4,4,64,512]{4,3,2,1,0:T(8,128)(2,1)}, u32[]{:S(2)}) copy-start(bf16[1,4,4,64,512]{4,3,2,1,0:T(8,128)(2,1)} %get-tuple-element.9) | copy-start | bytes 3145732
  57.0 1.2 %copy-start.7 = (bf16[1,4,4,64,512]{4,3,2,1,0:T(8,128)(2,1)S(1)}, bf16[1,4,4,64,512]{4,3,2,1,0:T(8,128)(2,1)}, u32[]{:S(2)}) copy-start(bf16[1,4,4,64,512]{4,3,2,1,0:T(8,128)(2,1)} %get-tuple-element.14) | copy-start | bytes 3145732
  57.7 1.3 %copy-start.5 = (bf16[1,4,4,64,512]{4,3,2,1,0:T(8,128)(2,1)S(1)}, bf16[1,4,4,64,512]{4,3,2,1,0:T(8,128)(2,1)}, u32[]{:S(2)}) copy-start(bf16[1,4,4,64,512]{4,3,2,1,0:T(8,128)(2,1)} %get-tuple-element.13) | copy-start | bytes 3145732
  59.7 0.7 copy-start.12
  78.5 1.6 %copy-start.9 = (bf16[1536,512]{1,0:T(8,128)(2,1)S(1)}, bf16[1536,512]{1,0:T(8,128)(2,1)}, u32[]{:S(2)}) copy-start(bf16[1536,512]{1,0:T(8,128)(2,1)} %all-gather.5.cloned.1.call-done) | copy-start | bytes 4718596
  80.6 1.6 %copy-start.2 = (f32[1,4,4,64,512]{4,3,2,1,0:T(8,128)S(1)}, f32[1,4,4,64,512]{4,3,2,1,0:T(8,128)}, u32[]{:S(2)}) copy-start(f32[1,4,4,64,512]{4,3,2,1,0:T(8,128)} %copy-done.1) | copy-start | bytes 6291460
  80.6 1.6 %copy-start.13 = (f32[512]{0:T(512)S(1)}, f32[512]{0:T(512)}, u32[]{:S(2)}) copy-start(f32[512]{0:T(512)} %param.13) | copy-start | bytes 6148
Sparse Core Ops, SparseCore 0:
  9.2 41.6 all-gather.2
  52.8 25.6 all-gather.4
where the time goes:
time: 91.8 us; the launch traced here: 91.4 us
  blocking collectives  21.8 us (24%)
  waiting for transfers between devices  21.7 us (24%)
  between operations  13.7 us (15%)
  matrix products  11.9 us (13%)
  other arithmetic  9.96 us (11%)
  local copies, waits for them, and re-layouts  7.12 us (8%)
  starting transfers between devices  5.22 us (6%)
    all_gather x1, waiting for transfers between devices, body(): lax.all_gather(temporal_weight, 'clip', axis=0, tiled=True)  16.6 us
    psum x1, blocking collectives, body(): group_mean = lax.psum(jnp.sum(grouped, axis=(1, 3)), 'row') / population  13.5 us
    dot_general x9, matrix products, body(): jnp.dot(window, spatial_full[tap_index * channels:(tap_index + 1) * chann...  9.46 us
    psum x1, blocking collectives, body(): lax.psum(jnp.sum(centered * centered, axis=(1, 3)), 'row') / population  8.37 us
    ppermute x1, waiting for transfers between devices, extended(): lax.ppermute(head, axis, [((i + 1) % count, i) for i in range(ends)])  4.4 us
    ppermute x1, starting transfers between devices, extended(): lax.ppermute(tail, axis, [(i, (i + 1) % count) for i in range(ends)])  3.89 us
    unnamed x32, local copies, waits for them, and re-layouts  3.23 us
    slice x1, local copies, waits for them, and re-layouts, body(): padded[:, :, row_shift:row_shift + row_count, col_shift:col_shift + col_c...  3.18 us
  transfers between devices with their start and end apart: 4, of which 2 were waited for; matrix products, arithmetic and copies ran while one was open for 23% of the time, Pallas kernels for 0%

commit v1 on v0

v1 whole, which is shorter than its diff:
```python
import functools

import jax
import jax.numpy as jnp
from jax import lax
from jax.experimental import pallas as pl
from jax.experimental.pallas import tpu as pltpu
from jax.sharding import PartitionSpec as P

GROUPS = 32
MESH = pl.DeviceIdType.MESH


def group_total(values, group_width):
    lanes = values.shape[1]
    step = 1
    while step < group_width:
        values = values + pltpu.roll(values, step, 1)
        step *= 2
    lane = lax.broadcasted_iota(jnp.int32, values.shape, 1)
    values = jnp.where(lane % group_width == group_width - 1, values, 0.0)
    step = 1
    while step < group_width:
        values = values + pltpu.roll(values, lanes - step, 1)
        step *= 2
    return values


def z_rows(rows):
    return max(rows // 64 * 16, 16)


def kernel(
    n_clip, n_row,
    x, gain, bias, spatial, spatial_bias, temporal, temporal_bias,
    out,
    spatial_full, temporal_full, act, acc, halo, stats,
    send_sems, recv_sems, local_sems,
):
    me, row = lax.axis_index("clip"), lax.axis_index("row")
    parity = row % 2
    _, frames, height, cols, channels = x.shape
    used = acc.shape[0]
    group_width = channels // GROUPS
    half = channels // 2
    bits = n_clip.bit_length() - 1
    chip_bits = [1 << k for k in range(1, bits)]
    orders = (chip_bits, chip_bits[::-1])
    own = (spatial, temporal)
    full = (spatial_full, temporal_full)

    def flip(index, mask):
        for k in range(bits):
            if mask >> k & 1:
                index = index + (1 - 2 * (index // (1 << k) % 2)) * (1 << k)
        return index

    sibling, layer = (flip(me, 1), row), (me, flip(row, 1))

    barrier = pltpu.get_barrier_semaphore()
    greeted = [(flip(me, 1 << k), row) for k in range(bits)]
    greeted += [(me, lax.rem(row + d, n_row)) for d in range(1, n_row)]
    for device in greeted:
        pl.semaphore_signal(barrier, inc=1, device_id=device, device_id_type=MESH)
    pl.semaphore_wait(barrier, len(greeted))

    arrivals, departures = {}, []

    def send(key, source, target, landing, device):
        slot = len(departures)
        copy = pltpu.make_async_remote_copy(
            src_ref=source, dst_ref=target, send_sem=send_sems.at[slot],
            recv_sem=recv_sems.at[slot], device_id=device, device_id_type=MESH,
        )
        copy.start()
        departures.append(copy)
        arrivals[key] = pltpu.make_async_remote_copy(
            src_ref=landing, dst_ref=landing, send_sem=send_sems.at[slot],
            recv_sem=recv_sems.at[slot], device_id=device, device_id_type=MESH,
        )

    def span(which, kind):
        rows = own[which].shape[0]
        edge = z_rows(rows)
        if kind == "mine":
            return parity * (rows - edge), edge
        if kind == "theirs":
            return (1 - parity) * (rows - edge), edge
        if kind == "direct":
            return edge, rows - 2 * edge
        return 0, rows

    def part(which, shard, kind, order=None):
        start, size = span(which, kind)
        base = pl.multiple_of(shard * own[which].shape[0] + start, 16)
        columns = slice(None) if order is None else pl.ds(order * half, half)
        return full[which].at[pl.ds(base, size), columns]

    def own_part(which, kind, order=None):
        start, size = span(which, kind)
        columns = slice(None) if order is None else pl.ds(order * half, half)
        if not isinstance(start, int):
            start = pl.multiple_of(start, 16)
        return own[which].at[pl.ds(start, size), columns]

    def hop(which, kind, order, stage, mask):
        bit = orders[order][stage]
        shard = flip(me, mask)
        source = own_part(which, kind, order) if mask == 0 else part(which, shard, kind, order)
        send(
            (which, kind, order, stage, mask), source, part(which, shard, kind, order),
            part(which, flip(shard, bit), kind, order), (flip(me, bit), row),
        )

    def send_own(which, kind):
        for stage in range(bits - 1):
            for order in range(2):
                hop(which, kind, order, stage, 0)

    def share(which, kind, mask):
        shard = flip(me, mask)
        source = part(which, shard, kind) if mask else own[which]
        send(
            (which, kind, "s", mask), source, part(which, shard, kind),
            part(which, flip(shard, 1), kind), sibling,
        )

    even_masks = range(2, n_clip, 2)

    def pump(which, kind, depth):
        for order in range(2):
            line = orders[order]
            for stage in range(bits - 1):
                earlier = sum(line[:stage])
                for mask in range(0, n_clip, 2):
                    gained = mask | line[stage]
                    if mask & ~earlier or gained.bit_count() != depth:
                        continue
                    arrivals[which, kind, order, stage, mask].wait_recv()
                    for later in range(stage + 1, bits - 1):
                        hop(which, kind, order, later, gained)
        for mask in even_masks:
            if mask.bit_count() == depth:
                if kind == "mine":
                    shard = flip(me, mask)
                    send(
                        (which, "z", mask), part(which, shard, "mine"),
                        part(which, shard, "mine"), part(which, shard, "theirs"), layer,
                    )
                share(which, kind, mask)

    def settle(which, depth):
        for mask in even_masks:
            if mask.bit_count() == depth:
                arrivals[which, "z", mask].wait_recv()
                share(which, "theirs", mask)

    def from_sibling(which, masks):
        for mask in masks:
            for kind in ("mine", "direct", "theirs") if mask else ("all",):
                arrivals[which, kind, "s", mask].wait_recv()

    def edge_copy(slot, source_row, target, device):
        return pltpu.make_async_remote_copy(
            src_ref=x.at[0, pl.ds(0, used), source_row], dst_ref=halo.at[target],
            send_sem=local_sems.at[2 + slot], recv_sem=local_sems.at[4 + slot],
            device_id=device, device_id_type=MESH,
        )

    down = edge_copy(0, height - 1, 0, (me, lax.rem(row + 1, n_row)))
    up = edge_copy(1, 0, 1, (me, lax.rem(row + n_row - 1, n_row)))
    has_above, has_below = row > 0, row < n_row - 1

    send_own(0, "mine")
    pl.when(has_below)(down.start)
    pl.when(has_above)(up.start)
    send_own(0, "direct")
    share(0, "all", 0)
    locals_ = [
        pltpu.make_async_copy(own[w], part(w, me, "all"), local_sems.at[w]) for w in range(2)
    ]
    for copy in locals_:
        copy.start()

    tiles = frames * height
    population = tiles * cols * group_width

    def tile(index):
        return x[0, index // height, index % height].astype(jnp.float32)

    def fold(values):
        return jnp.sum(values.reshape(cols // 8, 8, channels), axis=0)

    zeros = jnp.zeros((8, channels), jnp.float32)
    total = lax.fori_loop(0, tiles, lambda k, s: s + fold(tile(k)), zeros, unroll=2)
    total = jnp.broadcast_to(jnp.sum(total, axis=0, keepdims=True), (8, channels))
    near_mean = group_total(total, group_width) / population

    def squares(k, s):
        centred = tile(k) - near_mean[:1]
        return s + fold(centred * centred)

    square = lax.fori_loop(0, tiles, squares, zeros, unroll=2)
    square = jnp.broadcast_to(jnp.sum(square, axis=0, keepdims=True), (8, channels))
    near_square = group_total(square, group_width)
    line = lax.broadcasted_iota(jnp.int32, (8, channels), 0)
    stats[0] = jnp.where(line < 4, near_mean, near_square)
    for d in range(1, n_row):
        send(("stats", d), stats.at[0], stats.at[d], stats.at[d], (me, lax.rem(row + d, n_row)))

    pump(0, "mine", 1)
    send_own(1, "mine")

    for d in range(1, n_row):
        arrivals["stats", d].wait_recv()
    means = [stats[d, 0:1] for d in range(n_row)]
    mean = sum(means) / n_row
    spread = sum(stats[d, 4:5] for d in range(n_row))
    spread = spread + population * sum((m - mean) * (m - mean) for m in means)
    inverse = lax.rsqrt(spread / (population * n_row) + 1e-06)

    place = lax.broadcasted_iota(jnp.int32, (cols, channels), 0)

    def put(frame, line, values):
        for b, moved in enumerate((
            jnp.where(place == 0, 0.0, pltpu.roll(values, 1, 0)),
            values,
            jnp.where(place == cols - 1, 0.0, pltpu.roll(values, cols - 1, 0)),
        )):
            moved = moved.astype(jnp.bfloat16)
            for c in range(2):
                act[b, c, frame, line] = moved[:, c * half:(c + 1) * half]

    def activate(values):
        normed = (values - mean) * inverse * gain[...] + bias[...]
        return normed / (1.0 + jnp.exp(-normed))

    @pl.loop(0, used * height)
    def _(index):
        frame, line = index // height, index % height
        put(frame, line + 1, activate(x[0, frame, line].astype(jnp.float32)))

    pump(0, "direct", 1)
    send_own(1, "direct")
    share(1, "all", 0)
    for depth in range(2, bits):
        pump(0, "mine", depth)

    for present, copy, target in ((has_above, down, 0), (has_below, up, 1)):
        line = target * (height + 1)

        @pl.when(present)
        def _():
            copy.wait_recv()

            @pl.loop(0, used)
            def _(frame):
                put(frame, line, activate(halo[target, frame].astype(jnp.float32)))

        @pl.when(jnp.logical_not(present))
        def _():
            @pl.loop(0, used)
            def _(frame):
                for b in range(3):
                    for c in range(2):
                        act[b, c, frame, line] = jnp.zeros((cols, half), jnp.bfloat16)

    quarter = me // (n_clip // 4)

    def convolve(phase, blocks):
        @pl.loop(0, used)
        def _(frame):
            value = None
            for block in blocks:
                tap, c = block // 2, block % 2
                window = act[tap % 3, c, frame, pl.ds(tap // 3, height)]
                rows = pl.ds(pl.multiple_of(block * half, half), half)
                product = jnp.dot(
                    window.reshape(height * cols, half), spatial_full[rows, :],
                    preferred_element_type=jnp.float32,
                )
                value = product if value is None else value + product
            acc[frame] = value + (spatial_bias[...] if phase == 0 else acc[frame])

    def blocks_of(phase):
        spot = quarter
        if phase & 1:
            spot = spot + 1 - 2 * (spot % 2)
        if phase & 2:
            spot = (spot + 2) % 4
        first = (9 * spot + 1) // 2
        chosen = [first + k for k in range(4)]
        if phase & 1:
            chosen.append(spot // 2 * 9 + 4)
        return chosen

    def of_phase(phase):
        return [m for m in range(0, n_clip, 2) if m >> (bits - 2) == phase]

    locals_[0].wait()
    early = n_clip == 8
    if early:
        from_sibling(0, of_phase(0))
        convolve(0, blocks_of(0))
    pump(1, "mine", 1)
    for depth in range(2, bits):
        pump(0, "direct", depth)
    for depth in range(1, bits):
        settle(0, depth)
    pump(1, "direct", 1)
    for depth in range(2, bits):
        pump(1, "mine", depth)
    if not early:
        from_sibling(0, of_phase(0))
        convolve(0, blocks_of(0))
    for phase in (1, 2):
        from_sibling(0, of_phase(phase))
        convolve(phase, blocks_of(phase))
    for depth in range(2, bits):
        pump(1, "direct", depth)
    for depth in range(1, bits):
        settle(1, depth)
    from_sibling(0, of_phase(3))
    convolve(3, blocks_of(3))

    locals_[1].wait()
    from_sibling(1, range(0, n_clip, 2))

    def tap_product(k, frame):
        return jnp.dot(
            acc[frame].astype(jnp.bfloat16), temporal_full[k * channels:(k + 1) * channels, :],
            preferred_element_type=jnp.float32,
        )

    for j in range(frames // 2):
        before, at = max(2 * j - 1, 0), 2 * j
        pooled = 0.5 * (x[0, before].astype(jnp.float32) + x[0, at].astype(jnp.float32))
        value = sum(tap_product(k, max(2 * j + k - 2, 0)) for k in range(3))
        value = value + temporal_bias[...] + pooled.reshape(height * cols, channels)
        out[0, j] = value.reshape(height, cols, channels).astype(out.dtype)

    for copy in departures:
        copy.wait_send()
    pl.when(has_below)(down.wait_send)
    pl.when(has_above)(up.wait_send)


def body(
    n_clip, n_row,
    video_clips, norm_gain, norm_bias, spatial_weight, spatial_bias, temporal_weight, temporal_bias,
):
    _, frames, height, cols, channels = video_clips.shape
    used = frames - 1
    half = channels // 2
    shards = n_clip // 2 - 1
    copies = 2 * (4 * shards + shards + 3 * shards + 1) + n_row - 1
    vmem = pl.BlockSpec(memory_space=pltpu.VMEM)
    hbm = pl.BlockSpec(memory_space=pl.ANY)
    flat = lambda v: v.reshape(1, channels)
    return pl.pallas_call(
        functools.partial(kernel, n_clip, n_row),
        out_shape=jax.ShapeDtypeStruct((1, frames // 2, height, cols, channels), jnp.bfloat16),
        in_specs=[vmem, vmem, vmem, hbm, vmem, hbm, vmem],
        out_specs=vmem,
        scratch_shapes=[
            pltpu.VMEM((9 * channels, channels), jnp.bfloat16),
            pltpu.VMEM((3 * channels, channels), jnp.bfloat16),
            pltpu.VMEM((3, 2, used, height + 2, cols, half), jnp.bfloat16),
            pltpu.VMEM((used, height * cols, channels), jnp.float32),
            pltpu.VMEM((2, used, cols, channels), jnp.bfloat16),
            pltpu.VMEM((n_row, 8, channels), jnp.float32),
            pltpu.SemaphoreType.DMA((copies,)),
            pltpu.SemaphoreType.DMA((copies,)),
            pltpu.SemaphoreType.DMA((6,)),
        ],
        compiler_params=pltpu.CompilerParams(
            collective_id=0, has_side_effects=True, vmem_limit_bytes=40 * 1024 * 1024
        ),
    )(
        video_clips, flat(norm_gain), flat(norm_bias), spatial_weight, flat(spatial_bias),
        temporal_weight, flat(temporal_bias),
    )


def solution(mesh):
    placed = (
        P("clip", None, "row", None, None),
        P(),
        P(),
        P("clip", None),
        P(),
        P("clip", None),
        P(),
    )
    return jax.shard_map(
        functools.partial(body, mesh.shape["clip"], mesh.shape["row"]),
        mesh=mesh,
        in_specs=placed,
        out_specs=P("clip", None, "row", None, None),
        check_vma=False,
    )
```

time: 91.8 us -> 38 us (0.41)
  Pallas kernels: 0 us -> 32.3 us
  blocking collectives: 21.8 us -> 0 us
  waiting for transfers between devices: 21.7 us -> 0 us
  between operations: 13.7 us -> 0.02 us
  matrix products: 11.9 us -> 0 us
  other arithmetic: 9.96 us -> 0 us
  starting transfers between devices: 5.22 us -> 0 us
  local copies, waits for them, and re-layouts: 7.12 us -> 5.4 us
    pallas_call x0 -> x1, Pallas kernels: none -> 32.3 us  [body(): pl.pallas_call(functools.partial(kernel, n_clip, n_row), out_shape=jax.Sh...]
    psum x2 -> x0, blocking collectives: 21.8 us -> none  [the longest x1 13.5 us: body(): group_mean = lax.psum(jnp.sum(grouped, axis=(1, 3)), 'row') / population]
    all_gather x2 -> x0, waiting for transfers between devices: 16.6 us -> none  [the longest x1 16.6 us: body(): lax.all_gather(temporal_weight, 'clip', axis=0, tiled=True)]
    dot_general x12 -> x0, matrix products: 11.9 us -> none  [the longest x9 9.46 us: body(): jnp.dot(window, spatial_full[tap_index * channels:(tap_index + 1) * chann...]
    ppermute x2 -> x0, starting transfers between devices: 5.18 us -> none  [the longest x1 3.89 us: extended(): lax.ppermute(tail, axis, [(i, (i + 1) % count) for i in range(ends)])]
    concatenate x4 -> x0, other arithmetic: 4.52 us -> none  [the longest x2 2.47 us: extended(): jnp.concatenate([lax.ppermute(tail, axis, [(i, (i + 1) % count) for i in...]
    ppermute x2 -> x0, waiting for transfers between devices: 4.4 us -> none  [the longest x1 4.4 us: extended(): lax.ppermute(head, axis, [((i + 1) % count, i) for i in range(ends)])]
    slice x6 -> x0, local copies, waits for them, and re-layouts: 3.43 us -> none  [the longest x1 3.18 us: body(): padded[:, :, row_shift:row_shift + row_count, col_shift:col_shift + col_c...]
  transfers between devices with their start and end apart: 4 -> 0, of which waited for: 2 -> 0; matrix products, arithmetic and copies ran while one was open for 23% -> 0% of each run, Pallas kernels for 0% -> 0%
where the time goes in v1:
time: 38 us; the launch traced here: 37.7 us
  Pallas kernels  32.3 us (85%)
  local copies, waits for them, and re-layouts  5.4 us (14%)
    pallas_call x1, Pallas kernels, body(): pl.pallas_call(functools.partial(kernel, n_clip, n_row), out_shape=jax.Sh...  32.3 us
    unnamed x15, local copies, waits for them, and re-layouts  5.4 us

profile of v1, /device:TPU:0, one launch (start us, length us, event | category | flops | bytes accessed | tf_op | source)
XLA Modules:
  0.0 37.7 jit_solution(13508998194495329993)
XLA Ops:
  0.0 0.0 copy-start.5
  0.0 0.0 copy-start.4
  0.0 0.0 copy-start.3
  0.0 0.7 %copy-done.5 = f32[512]{0:T(512)S(1)} copy-done((f32[512]{0:T(512)S(1)}, f32[512]{0:T(512)}, u32[]{:S(2)}) %copy-start.5) | copy-done | bytes 2072
  0.7 0.0 copy-done.4
  0.7 0.0 copy-done.3
  0.7 0.0 copy-start
  0.7 1.2 %copy-done = bf16[1,4,4,64,512]{4,3,2,1,0:T(8,128)(2,1)S(1)} copy-done((bf16[1,4,4,64,512]{4,3,2,1,0:T(8,128)(2,1)S(1)}, bf16[1,4,4,64,512]{4,3,2,1,0:T(8,128)(2,1)}, u32[]{:S(2)}) %copy-start) | copy-done | bytes 1048600
  1.9 0.0 copy-start.1
  1.9 1.1 %copy-done.1 = bf16[576,512]{1,0:T(8,128)(2,1)S(1)} copy-done((bf16[576,512]{1,0:T(8,128)(2,1)S(1)}, bf16[576,512]{1,0:T(8,128)(2,1)}, u32[]{:S(2)}) %copy-start.1) | copy-done | bytes 589848
  3.0 0.0 copy-start.2
  3.0 0.9 %copy-done.2 = bf16[192,512]{1,0:T(8,128)(2,1)S(1)} copy-done((bf16[192,512]{1,0:T(8,128)(2,1)S(1)}, bf16[192,512]{1,0:T(8,128)(2,1)}, u32[]{:S(2)}) %copy-start.2) | copy-done | bytes 196632
  3.9 0.0 copy-start.6
  3.9 0.7 %copy-done.6 = f32[512]{0:T(512)S(1)} copy-done((f32[512]{0:T(512)S(1)}, f32[512]{0:T(512)}, u32[]{:S(2)}) %copy-start.6) | copy-done | bytes 2072
  4.6 32.3 %shard_map.73 = bf16[1,2,4,64,512]{4,3,2,1,0:T(8,128)(2,1)S(1)} custom-call(bf16[1,4,4,64,512]{4,3,2,1,0:T(8,128)(2,1)S(1)} %copy-done, f32[1,512]{1,0:T(1,128)S(1)} %bitcast.4, f32[1,512]{1,0:T(1,128)S(1)} %bitcast.5, bf16[576,512]{1,0:T(8,128)(2,1)S(1)} %copy-done.1, f32[1,512]{1,0:T(1,128)S(1)} %bitcast.6, bf16[192,512]{1,0:T(8,128)(2,1)S(1)} %copy-done.2, ...), custom_call_target="tpu_custom_call" | custom-call | tf_op jit(solution)/shard_map/pallas_call | solution.py:360
  36.9 0.8 %copy.9 = bf16[1,2,4,64,512]{4,3,2,1,0:T(8,128)(2,1)} copy(bf16[1,2,4,64,512]{4,3,2,1,0:T(8,128)(2,1)S(1)} %shard_map.73) | data formatting | bytes 1048576
Async XLA Ops:
  0.0 0.7 %copy-start.5 = (f32[512]{0:T(512)S(1)}, f32[512]{0:T(512)}, u32[]{:S(2)}) copy-start(f32[512]{0:T(512)} %param.11) | copy-start | bytes 6148
  0.0 0.7 %copy-start.4 = (f32[512]{0:T(512)S(1)}, f32[512]{0:T(512)}, u32[]{:S(2)}) copy-start(f32[512]{0:T(512)} %param.9) | copy-start | bytes 6148
  0.0 0.7 %copy-start.3 = (f32[512]{0:T(512)S(1)}, f32[512]{0:T(512)}, u32[]{:S(2)}) copy-start(f32[512]{0:T(512)} %param.8) | copy-start | bytes 6148
  0.7 1.2 %copy-start = (bf16[1,4,4,64,512]{4,3,2,1,0:T(8,128)(2,1)S(1)}, bf16[1,4,4,64,512]{4,3,2,1,0:T(8,128)(2,1)}, u32[]{:S(2)}) copy-start(bf16[1,4,4,64,512]{4,3,2,1,0:T(8,128)(2,1)} %x.1) | copy-start | bytes 3145732
  1.9 1.1 %copy-start.1 = (bf16[576,512]{1,0:T(8,128)(2,1)S(1)}, bf16[576,512]{1,0:T(8,128)(2,1)}, u32[]{:S(2)}) copy-start(bf16[576,512]{1,0:T(8,128)(2,1)} %spatial.1) | copy-start | bytes 1769476
  3.0 0.9 %copy-start.2 = (bf16[192,512]{1,0:T(8,128)(2,1)S(1)}, bf16[192,512]{1,0:T(8,128)(2,1)}, u32[]{:S(2)}) copy-start(bf16[192,512]{1,0:T(8,128)(2,1)} %temporal.1) | copy-start | bytes 589828
  3.9 0.7 %copy-start.6 = (f32[512]{0:T(512)S(1)}, f32[512]{0:T(512)}, u32[]{:S(2)}) copy-start(f32[512]{0:T(512)} %param.13) | copy-start | bytes 6148

commit v2 on v1

--- a/solution.py
+++ b/solution.py
@@ -32,14 +32,15 @@
 
 def kernel(
     n_clip, n_row,
-    x, gain, bias, spatial, spatial_bias, temporal, temporal_bias,
+    clips, gain_in, bias_in, spatial, spatial_bias_in, temporal, temporal_bias_in,
     out,
+    x, gain, bias, spatial_bias, temporal_bias,
     spatial_full, temporal_full, act, acc, halo, stats,
     send_sems, recv_sems, local_sems,
 ):
     me, row = lax.axis_index("clip"), lax.axis_index("row")
     parity = row % 2
-    _, frames, height, cols, channels = x.shape
+    _, frames, height, cols, channels = clips.shape
     used = acc.shape[0]
     group_width = channels // GROUPS
     half = channels // 2
@@ -56,6 +57,18 @@
         return index
 
     sibling, layer = (flip(me, 1), row), (me, flip(row, 1))
+
+    fetch = pltpu.make_async_copy(clips, x, local_sems.at[6])
+    fetch.start()
+    vectors = [
+        pltpu.make_async_copy(source, target, local_sems.at[7 + k])
+        for k, (source, target) in enumerate((
+            (gain_in, gain), (bias_in, bias),
+            (spatial_bias_in, spatial_bias), (temporal_bias_in, temporal_bias),
+        ))
+    ]
+    for copy in vectors:
+        copy.start()
 
     barrier = pltpu.get_barrier_semaphore()
     greeted = [(flip(me, 1 << k), row) for k in range(bits)]
@@ -162,7 +175,7 @@
 
     def edge_copy(slot, source_row, target, device):
         return pltpu.make_async_remote_copy(
-            src_ref=x.at[0, pl.ds(0, used), source_row], dst_ref=halo.at[target],
+            src_ref=clips.at[0, pl.ds(0, used), source_row], dst_ref=halo.at[target],
             send_sem=local_sems.at[2 + slot], recv_sem=local_sems.at[4 + slot],
             device_id=device, device_id_type=MESH,
         )
@@ -181,6 +194,10 @@
     ]
     for copy in locals_:
         copy.start()
+
+    fetch.wait()
+    for copy in vectors:
+        copy.wait()
 
     tiles = frames * height
     population = tiles * cols * group_width
@@ -360,9 +377,14 @@
     return pl.pallas_call(
         functools.partial(kernel, n_clip, n_row),
         out_shape=jax.ShapeDtypeStruct((1, frames // 2, height, cols, channels), jnp.bfloat16),
-        in_specs=[vmem, vmem, vmem, hbm, vmem, hbm, vmem],
+        in_specs=[hbm] * 7,
         out_specs=vmem,
         scratch_shapes=[
+            pltpu.VMEM((1, frames, height, cols, channels), jnp.bfloat16),
+            pltpu.VMEM((1, channels), jnp.float32),
+            pltpu.VMEM((1, channels), jnp.float32),
+            pltpu.VMEM((1, channels), jnp.float32),
+            pltpu.VMEM((1, channels), jnp.float32),
             pltpu.VMEM((9 * channels, channels), jnp.bfloat16),
             pltpu.VMEM((3 * channels, channels), jnp.bfloat16),
             pltpu.VMEM((3, 2, used, height + 2, cols, half), jnp.bfloat16),
@@ -371,10 +393,10 @@
             pltpu.VMEM((n_row, 8, channels), jnp.float32),
             pltpu.SemaphoreType.DMA((copies,)),
             pltpu.SemaphoreType.DMA((copies,)),
-            pltpu.SemaphoreType.DMA((6,)),
+            pltpu.SemaphoreType.DMA((11,)),
         ],
         compiler_params=pltpu.CompilerParams(
-            collective_id=0, has_side_effects=True, vmem_limit_bytes=40 * 1024 * 1024
+            collective_id=0, has_side_effects=True, vmem_limit_bytes=60 * 1024 * 1024
         ),
     )(
         video_clips, flat(norm_gain), flat(norm_bias), spatial_weight, flat(spatial_bias),

time: 38 us -> 35.4 us (0.932)
  local copies, waits for them, and re-layouts: 5.4 us -> 1.87 us
  Pallas kernels: 32.3 us -> 33.4 us
    unnamed x15 -> x1, local copies, waits for them, and re-layouts: 5.4 us -> 1.87 us
    pallas_call x1, Pallas kernels: 32.3 us -> 33.4 us  [body(): pl.pallas_call(functools.partial(kernel, n_clip, n_row), out_shape=jax.Sh...]
where the time goes in v2:
time: 35.4 us; the launch traced here: 35.3 us
  Pallas kernels  33.4 us (94%)
  local copies, waits for them, and re-layouts  1.87 us (5%)
    pallas_call x1, Pallas kernels, body(): pl.pallas_call(functools.partial(kernel, n_clip, n_row), out_shape=jax.Sh...  33.4 us
    unnamed x1, local copies, waits for them, and re-layouts  1.87 us

profile of v2, /device:TPU:0, one launch (start us, length us, event | category | flops | bytes accessed | tf_op | source)
XLA Modules:
  0.0 35.3 jit_solution(10636056276263044202)
XLA Ops:
  0.0 33.4 %shard_map.73 = bf16[1,2,4,64,512]{4,3,2,1,0:T(8,128)(2,1)} custom-call(bf16[1,4,4,64,512]{4,3,2,1,0:T(8,128)(2,1)} %clips.1, f32[1,512]{1,0:T(1,128)} %bitcast.4, f32[1,512]{1,0:T(1,128)} %bitcast.5, bf16[576,512]{1,0:T(8,128)(2,1)} %spatial.1, f32[1,512]{1,0:T(1,128)} %bitcast.6, bf16[192,512]{1,0:T(8,128)(2,1)} %temporal.1, f32[1,512]{1,0:T(1,128)} %bitcast.7), custom_call_target="tpu_custom_call" | custom-call | tf_op jit(solution)/shard_map/pallas_call | solution.py:377
  33.4 1.9 %copy.9 = bf16[1,2,4,64,512]{4,3,2,1,0:T(8,128)(2,1)} copy(bf16[1,2,4,64,512]{4,3,2,1,0:T(8,128)(2,1)} %shard_map.73) | data formatting | bytes 1048576

commit v3 on v2

--- a/solution.py
+++ b/solution.py
@@ -36,7 +36,7 @@
     out,
     x, gain, bias, spatial_bias, temporal_bias,
     spatial_full, temporal_full, act, acc, halo, stats,
-    send_sems, recv_sems, local_sems,
+    send_sems, recv_sems, local_sems, stat_sends, stat_recvs,
 ):
     me, row = lax.axis_index("clip"), lax.axis_index("row")
     parity = row % 2
@@ -72,10 +72,19 @@
 
     barrier = pltpu.get_barrier_semaphore()
     greeted = [(flip(me, 1 << k), row) for k in range(bits)]
-    greeted += [(me, lax.rem(row + d, n_row)) for d in range(1, n_row)]
+    has_above, has_below = row > 0, row < n_row - 1
+    above, below = (me, lax.rem(row + n_row - 1, n_row)), (me, lax.rem(row + 1, n_row))
+
+    def greet(device):
+        pl.semaphore_signal(barrier, inc=1, device_id=device, device_id_type=MESH)
+
     for device in greeted:
-        pl.semaphore_signal(barrier, inc=1, device_id=device, device_id_type=MESH)
-    pl.semaphore_wait(barrier, len(greeted))
+        greet(device)
+    pl.when(has_above)(lambda: greet(above))
+    pl.when(has_below)(lambda: greet(below))
+    pl.semaphore_wait(
+        barrier, len(greeted) + has_above.astype(jnp.int32) + has_below.astype(jnp.int32)
+    )
 
     arrivals, departures = {}, []
 
@@ -180,9 +189,8 @@
             device_id=device, device_id_type=MESH,
         )
 
-    down = edge_copy(0, height - 1, 0, (me, lax.rem(row + 1, n_row)))
-    up = edge_copy(1, 0, 1, (me, lax.rem(row + n_row - 1, n_row)))
-    has_above, has_below = row > 0, row < n_row - 1
+    down = edge_copy(0, height - 1, 0, below)
+    up = edge_copy(1, 0, 1, above)
 
     send_own(0, "mine")
     pl.when(has_below)(down.start)
@@ -221,15 +229,38 @@
     square = jnp.broadcast_to(jnp.sum(square, axis=0, keepdims=True), (8, channels))
     near_square = group_total(square, group_width)
     line = lax.broadcasted_iota(jnp.int32, (8, channels), 0)
-    stats[0] = jnp.where(line < 4, near_mean, near_square)
-    for d in range(1, n_row):
-        send(("stats", d), stats.at[0], stats.at[d], stats.at[d], (me, lax.rem(row + d, n_row)))
+    stats[row] = jnp.where(line < 4, near_mean, near_square)
+
+    def passing(way, k, source):
+        slot = way * (n_row - 1) + k
+        where = stats.at[lax.rem(source + n_row, n_row)]
+        return pltpu.make_async_remote_copy(
+            src_ref=where, dst_ref=where, send_sem=stat_sends.at[slot],
+            recv_sem=stat_recvs.at[slot], device_id=(below, above)[way], device_id_type=MESH,
+        )
+
+    goes, comes = [], []
+    for k in range(n_row - 1):
+        goes.append((
+            (jnp.logical_and(row >= k, has_below), passing(0, k, row - k)),
+            (jnp.logical_and(row + k < n_row, has_above), passing(1, k, row + k)),
+        ))
+        comes.append((
+            (row - 1 - k >= 0, passing(0, k, row - 1 - k)),
+            (row + 1 + k < n_row, passing(1, k, row + 1 + k)),
+        ))
+    for present, copy in goes[0]:
+        pl.when(present)(copy.start)
 
     pump(0, "mine", 1)
     send_own(1, "mine")
 
-    for d in range(1, n_row):
-        arrivals["stats", d].wait_recv()
+    for k in range(n_row - 1):
+        for present, copy in comes[k]:
+            pl.when(present)(copy.wait_recv)
+        if k + 1 < n_row - 1:
+            for present, copy in goes[k + 1]:
+                pl.when(present)(copy.start)
     means = [stats[d, 0:1] for d in range(n_row)]
     mean = sum(means) / n_row
     spread = sum(stats[d, 4:5] for d in range(n_row))
@@ -358,6 +389,9 @@
 
     for copy in departures:
         copy.wait_send()
+    for pair in goes:
+        for present, copy in pair:
+            pl.when(present)(copy.wait_send)
     pl.when(has_below)(down.wait_send)
     pl.when(has_above)(up.wait_send)
 
@@ -370,7 +404,7 @@
     used = frames - 1
     half = channels // 2
     shards = n_clip // 2 - 1
-    copies = 2 * (4 * shards + shards + 3 * shards + 1) + n_row - 1
+    copies = 2 * (4 * shards + shards + 3 * shards + 1)
     vmem = pl.BlockSpec(memory_space=pltpu.VMEM)
     hbm = pl.BlockSpec(memory_space=pl.ANY)
     flat = lambda v: v.reshape(1, channels)
@@ -394,6 +428,8 @@
             pltpu.SemaphoreType.DMA((copies,)),
             pltpu.SemaphoreType.DMA((copies,)),
             pltpu.SemaphoreType.DMA((11,)),
+            pltpu.SemaphoreType.DMA((2 * (n_row - 1),)),
+            pltpu.SemaphoreType.DMA((2 * (n_row - 1),)),
         ],
         compiler_params=pltpu.CompilerParams(
             collective_id=0, has_side_effects=True, vmem_limit_bytes=60 * 1024 * 1024

time: 35.4 us -> 34.6 us (0.977)
  Pallas kernels: 33.4 us -> 32.6 us
    pallas_call x1, Pallas kernels: 33.4 us -> 32.6 us  [body(): pl.pallas_call(functools.partial(kernel, n_clip, n_row), out_shape=jax.Sh...]
where the time goes in v3:
time: 34.6 us; the launch traced here: 34.4 us
  Pallas kernels  32.6 us (94%)
  local copies, waits for them, and re-layouts  1.87 us (5%)
    pallas_call x1, Pallas kernels, body(): pl.pallas_call(functools.partial(kernel, n_clip, n_row), out_shape=jax.Sh...  32.6 us
    unnamed x1, local copies, waits for them, and re-layouts  1.87 us

profile of v3, /device:TPU:0, one launch (start us, length us, event | category | flops | bytes accessed | tf_op | source)
XLA Modules:
  0.0 34.4 jit_solution(5056288595310798409)
XLA Ops:
  0.0 32.6 %shard_map.73 = bf16[1,2,4,64,512]{4,3,2,1,0:T(8,128)(2,1)} custom-call(bf16[1,4,4,64,512]{4,3,2,1,0:T(8,128)(2,1)} %clips.1, f32[1,512]{1,0:T(1,128)} %bitcast.4, f32[1,512]{1,0:T(1,128)} %bitcast.5, bf16[576,512]{1,0:T(8,128)(2,1)} %spatial.1, f32[1,512]{1,0:T(1,128)} %bitcast.6, bf16[192,512]{1,0:T(8,128)(2,1)} %temporal.1, f32[1,512]{1,0:T(1,128)} %bitcast.7), custom_call_target="tpu_custom_call" | custom-call | tf_op jit(solution)/shard_map/pallas_call | solution.py:411
  32.6 1.9 %copy.9 = bf16[1,2,4,64,512]{4,3,2,1,0:T(8,128)(2,1)} copy(bf16[1,2,4,64,512]{4,3,2,1,0:T(8,128)(2,1)} %shard_map.73) | data formatting | bytes 1048576
